TPU v7x, 32 devices: a whole 2x2x4 slice. The times are simulated.
32 devices in a mesh: ctx: 8 (over z, x), head: 4 (over y, core).
Axes of the slice: x: 2, y: 2, z: 4, core: 2. Of those that a mesh axis runs over, the one named last changes fastest.
Arguments:
- lin_query: bfloat16 [3072, 8192], P('ctx', 'head'), may hold values from -4 to 4
- lin_key: bfloat16 [3072, 8192], P('ctx', 'head'), may hold values from -4 to 4
- lin_value: bfloat16 [3072, 8192], P('ctx', 'head'), may hold values from -400 to 400
- lin_gate: bfloat16 [3072, 8192], P('ctx', 'head'), may hold values from -8 to 8
- lin_decay: float32 [3072, 64], P('ctx', 'head'), may hold values from -1 to 0
- norm_gain: float32 [8192], P('head'), may hold values from 0.25 to 1.75
- soft_query: bfloat16 [3072, 8192], P('ctx', 'head'), may hold values from -6.5 to 6.5
- soft_key: bfloat16 [3072, 1024], P('ctx', 'head'), may hold values from -6.5 to 6.5
- soft_value: bfloat16 [3072, 1024], P('ctx', 'head'), may hold values from -6 to 6
- starts: int32 [4], replicated, may hold values from 1 to 2400, as said below
- lengths: int32 [4], replicated, may hold values from 384 to 768, as said below
Outputs:
- lin_out: bfloat16 [3072, 8192], P('ctx', 'head')
- soft_out: bfloat16 [3072, 8192], P('ctx', 'head')
Inputs may be any that keep to these rules, and one draw needn't show every extreme that they name: `starts`: sequence s begins 1 to min(96, 192) positions after s * 768; sequences 1 and 2 begin at the same offset, no sequence runs into the next, and the last one ends at the pack's end. `lengths`: sequence 1 has length 768 in every draw.
All inputs are finite; a program needn't handle non-finite values.
Results may differ from a plain program's by a relative error of at most 0.012.
Values may be sent and summed in bfloat16 or wider, within the bound.
A program may use at most 128 MiB of HBM per device.

v0:
```python
import jax
import jax.numpy as jnp
from jax import lax
from jax.sharding import PartitionSpec as P

neg_big = -1e30
norm_eps = 1e-06


def passed_along(block, axis, distance):
    devices = range(lax.axis_size(axis))
    route = [(i - distance, i) for i in devices if i - distance in devices]
    return lax.ppermute(block, axis, route)


def segment_info(positions, starts, lengths):
    begun = (starts[None, :] <= positions[:, None]).astype(jnp.int32)
    segment = jnp.sum(begun, axis=1) - 1
    picked = jnp.arange(starts.shape[0], dtype=jnp.int32)[None, :] == segment[:, None]
    seg_start = jnp.sum(jnp.where(picked, starts[None, :], 0), axis=1)
    seg_length = jnp.sum(jnp.where(picked, lengths[None, :], 0), axis=1)
    valid = (segment >= 0) & (positions < seg_start + seg_length)
    return (segment, valid)


def lightning_local(query, keys, values, decay, segment, valid, before):
    row_count = query.shape[0]
    cumulative = jnp.cumsum(decay, axis=0)
    row_order = jnp.arange(row_count)
    visible = (
        (row_order[None, :] <= row_order[:, None])
        & (segment[None, :] == segment[:, None])
        & valid[None, :]
    )
    by_head = jnp.transpose(cumulative)
    log_gap = by_head[:, :, None] - by_head[:, None, :]
    factor = jnp.where(visible[None], jnp.exp(jnp.where(visible[None], log_gap, 0.0)), 0.0)
    scores = jnp.einsum("thd,shd->hts", query, keys, preferred_element_type=jnp.float32)
    weights = (scores * factor).astype(jnp.bfloat16)
    intra = jnp.einsum("hts,shd->thd", weights, values, preferred_element_type=jnp.float32)
    enter = jnp.exp(cumulative) * (segment == before).astype(jnp.float32)[:, None]
    end_ok = ((segment == segment[-1]) & valid).astype(jnp.float32)
    to_end = jnp.exp(cumulative[-1][None, :] - cumulative) * end_ok[:, None]
    decay_total = jnp.exp(cumulative[-1]) * (segment[-1] == before).astype(jnp.float32)
    local_state = jnp.einsum(
        "thd,the->hde",
        keys.astype(jnp.float32) * to_end[:, :, None],
        values.astype(jnp.float32),
        precision=lax.Precision.HIGHEST,
    )
    return (intra, enter, decay_total, local_state)


def join_states(earlier, later):
    decay_early, state_early = earlier
    decay_late, state_late = later
    return (decay_early * decay_late, decay_late[:, None, None] * state_early + state_late)


def rows_last(scale):
    return jnp.moveaxis(scale, -1, 0)[..., None]


def attend(state, query, query_pos, query_seg, keys, values, key_pos, key_seg, key_valid):
    running_max, running_sum, weighted = state
    score_scale = query.shape[3] ** (-0.5)
    scores = (
        jnp.einsum("qkgd,skd->kgqs", query, keys, preferred_element_type=jnp.float32) * score_scale
    )
    visible = (
        (key_pos[None, :] <= query_pos[:, None])
        & (key_seg[None, :] == query_seg[:, None])
        & key_valid[None, :]
    )[None, None]
    masked = jnp.where(visible, scores, neg_big)
    new_max = jnp.maximum(running_max, jnp.max(masked, axis=3))
    shrink = jnp.exp(running_max - new_max)
    probs = jnp.where(visible, jnp.exp(masked - new_max[..., None]), 0.0)
    running_sum = running_sum * shrink + jnp.sum(probs, axis=3)
    update = jnp.einsum(
        "kgqs,skd->qkgd", probs.astype(jnp.bfloat16), values, preferred_element_type=jnp.float32
    )
    weighted = weighted * rows_last(shrink) + update
    return (new_max, running_sum, weighted)


def start_state(kv_count, group, row_count, head_dim):
    return (
        jnp.full((kv_count, group, row_count), neg_big, jnp.float32),
        jnp.zeros((kv_count, group, row_count), jnp.float32),
        jnp.zeros((row_count, kv_count, group, head_dim), jnp.float32),
    )


def finish(state, valid):
    final_max, final_sum, final_acc = state
    safe = jnp.where(valid[None, None, :], final_sum, 1.0)
    return final_acc / rows_last(safe) * valid.astype(jnp.float32)[:, None, None, None]


def per_device(
    lin_query,
    lin_key,
    lin_value,
    lin_gate,
    lin_decay,
    norm_gain,
    soft_query,
    soft_key,
    soft_value,
    starts,
    lengths,
):
    row_count = lin_query.shape[0]
    head_count = lin_decay.shape[1]
    features = lin_query.shape[1]
    head_dim = features // head_count
    kv_count = soft_key.shape[1] // head_dim
    group = head_count // kv_count
    device = lax.axis_index("ctx")
    window = lax.axis_size("ctx") // starts.shape[0]
    first = device * row_count
    row_ids = jnp.arange(row_count, dtype=jnp.int32)
    positions = first + row_ids
    segment, valid = segment_info(positions, starts, lengths)
    before, unused = segment_info(jnp.reshape(first - 1, (1,)), starts, lengths)
    query_lin = lin_query.reshape(row_count, head_count, head_dim)
    keys_lin = lin_key.reshape(row_count, head_count, head_dim)
    values_lin = lin_value.reshape(row_count, head_count, head_dim)
    intra, enter, decay_total, local_state = lightning_local(
        query_lin, keys_lin, values_lin, lin_decay, segment, valid, before[0]
    )
    identity = (
        jnp.ones((head_count,), jnp.float32),
        jnp.zeros((head_count, head_dim, head_dim), jnp.float32),
    )

    def relay_step(step, carried):
        joined = join_states(carried, (decay_total, local_state))
        return (
            passed_along(joined[0].astype(jnp.bfloat16), "ctx", 1).astype(jnp.float32),
            passed_along(joined[1].astype(jnp.bfloat16), "ctx", 1).astype(jnp.float32),
        )

    unused_decay, state_in = lax.fori_loop(0, window, relay_step, identity)
    carried_term = jnp.einsum(
        "thd,hde->the",
        query_lin.astype(jnp.float32) * enter[:, :, None],
        state_in,
        precision=lax.Precision.HIGHEST,
    )
    lin_heads = (intra + carried_term) * valid.astype(jnp.float32)[:, None, None]
    flat = lin_heads.reshape(row_count, features)
    square_sum = lax.psum(jnp.sum(flat * flat, axis=1), "head")
    mean_square = square_sum / (features * lax.axis_size("head"))
    lin_out = (
        flat
        * lax.rsqrt(mean_square + norm_eps)[:, None]
        * norm_gain[None, :]
        * jax.nn.sigmoid(lin_gate.astype(jnp.float32))
    ).astype(jnp.bfloat16)
    keys_soft = soft_key.reshape(row_count, kv_count, head_dim)
    values_soft = soft_value.reshape(row_count, kv_count, head_dim)

    def key_marks(owner):
        key_pos = owner * row_count + row_ids
        key_seg, key_valid = segment_info(key_pos, starts, lengths)
        return (key_pos, key_seg, key_valid)

    query_soft = soft_query.reshape(row_count, kv_count, group, head_dim)
    initial = start_state(kv_count, group, row_count, head_dim)
    own_pos, own_seg, own_valid = key_marks(device)
    state = attend(
        initial, query_soft, positions, segment, keys_soft, values_soft, own_pos, own_seg, own_valid
    )
    for distance in range(1, window + 1):
        far_keys, far_values = passed_along((keys_soft, values_soft), "ctx", distance)
        key_pos, key_seg, key_valid = key_marks(device - distance)
        state = attend(
            state, query_soft, positions, segment, far_keys, far_values, key_pos, key_seg, key_valid
        )
    soft_out = finish(state, valid).reshape(row_count, features).astype(jnp.bfloat16)
    return (lin_out, soft_out)


def solution(mesh):
    placed = (
        P("ctx", "head"),
        P("ctx", "head"),
        P("ctx", "head"),
        P("ctx", "head"),
        P("ctx", "head"),
        P("head"),
        P("ctx", "head"),
        P("ctx", "head"),
        P("ctx", "head"),
        P(),
        P(),
    )
    return jax.shard_map(
        per_device,
        mesh=mesh,
        in_specs=placed,
        out_specs=(P("ctx", "head"), P("ctx", "head")),
        check_vma=False,
    )
```

profile of v0, /device:TPU:12, one launch (start us, length us, event | category | flops | bytes accessed | tf_op | source)
XLA Modules:
  0.0 142.8 jit_solution(17728607761987084203)
XLA Ops:
  0.6 0.0 copy-start
  0.6 0.0 copy-start.6
  0.7 0.0 copy-start.7
  0.7 0.0 copy-start.4
  0.7 1.2 copy.86
  1.9 0.8 copy.92
  2.7 3.5 %collective-permute-start.3 = (bf16[384,2,128]{2,0,1:T(8,128)(2,1)}, bf16[384,2,128]{2,0,1:T(8,128)(2,1)}, u32[]{:S(2)}, u32[]{:S(2)}) collective-permute-start(bf16[384,2,128]{2,0,1:T(8,128)(2,1)} %copy.92), channel_id=1, source_target_pairs={{0,8},{4,12},{8,16},{12,20},{16,24},{20,28},{1,9},{5,13},{9,17},{1... | collective-permute-start | bytes 589832 | tf_op jit(solution)/shard_map/ppermute | solution.py:13
  6.2 3.4 %collective-permute-start.1 = (bf16[384,2,128]{2,0,1:T(8,128)(2,1)}, bf16[384,2,128]{2,0,1:T(8,128)(2,1)}, u32[]{:S(2)}, u32[]{:S(2)}) collective-permute-start(bf16[384,2,128]{2,0,1:T(8,128)(2,1)} %copy.92), channel_id=1, source_target_pairs={{0,4},{4,8},{8,12},{12,16},{16,20},{20,24},{24,28},{1,5},{5,9},{9,... | collective-permute-start | bytes 589832 | tf_op jit(solution)/shard_map/ppermute | solution.py:13
  9.6 1.7 %copy.89 = bf16[384,256]{0,1:T(8,128)(2,1)} copy(bf16[384,256]{1,0:T(8,128)(2,1)} %param.21) | data formatting | bytes 393216 | tf_op args[8]
  11.4 3.4 %collective-permute-start.2 = (bf16[384,2,128]{0,2,1:T(8,128)(2,1)}, bf16[384,2,128]{0,2,1:T(8,128)(2,1)}, u32[]{:S(2)}, u32[]{:S(2)}) collective-permute-start(bf16[384,2,128]{0,2,1:T(8,128)(2,1)} %bitcast.10), channel_id=1, source_target_pairs={{0,4},{4,8},{8,12},{12,16},{16,20},{20,24},{24,28},{1,5},{5,9},{9,... | collective-permute-start | bytes 589832 | tf_op jit(solution)/shard_map/ppermute | solution.py:13
  14.8 1.9 %collective-permute-start.4 = (bf16[384,2,128]{0,2,1:T(8,128)(2,1)}, bf16[384,2,128]{0,2,1:T(8,128)(2,1)}, u32[]{:S(2)}, u32[]{:S(2)}) collective-permute-start(bf16[384,2,128]{0,2,1:T(8,128)(2,1)} %bitcast.10), channel_id=1, source_target_pairs={{0,8},{4,12},{8,16},{12,20},{16,24},{20,28},{1,9},{5,13},{9,17},{1... | collective-permute-start | bytes 589832 | tf_op jit(solution)/shard_map/ppermute | solution.py:13
  16.8 0.8 convert_reduce_fusion
  17.6 1.3 fusion.75
  19.6 3.0 %copy.117 = bf16[48,8,16,128]{3,2,1,0:T(8,128)(2,1)} copy(bf16[48,8,16,128]{3,1,2,0:T(8,128)(2,1)} %bitcast.218) | data formatting | bytes 3145728
  22.5 0.6 slice.17
  23.8 0.0 copy-done.6
  23.8 0.0 copy-done.7
  23.8 0.1 select_reduce_fusion.4
  23.9 0.7 and_convert_fusion
  24.6 1.3 fusion.60
  25.9 0.3 copy.85
  26.2 0.0 copy-done.4
  26.2 0.9 reduce-window.6
  27.1 0.2 slice_reduce_fusion
  27.3 0.1 copy_bitcast_fusion
  27.4 0.2 slice_reduce_fusion.1
  27.6 2.6 %copy.112 = bf16[384,2048]{0,1:T(8,128)(2,1)} copy(bf16[384,2048]{1,0:T(8,128)(2,1)} %param.14) | data formatting | bytes 3145728 | tf_op jit(solution)/shard_map/reshape | solution.py:128
  30.2 0.1 exponential_multiply_fusion
  30.3 4.6 %fusion.36 = f32[16,128,128]{2,1,0:T(8,128)} fusion(bf16[384,16,128]{0,2,1:T(8,128)(2,1)} %bitcast.213, f32[384,16]{0,1:T(8,128)S(1)} %get-tuple-element.81, bf16[384,2048]{1,0:T(8,128)(2,1)} %param.15), kind=kOutput, calls=%fused_computation.46 | convolution fusion | flops 1209532416 | bytes 4218880 | tf_op jit(solution)/shard_map/thd,the->hde/dot_general | solution.py:45
  34.9 36.3 %while.11 = (s32[]{:T(128)}, f32[16,128,128]{2,1,0:T(8,128)S(1)}, f32[16]{0:T(128)S(1)}, f32[16,128,128]{2,1,0:T(8,128)}, s32[]{:T(128)}, /*index=5*/s32[]{:T(128)}) while((s32[]{:T(128)}, f32[16,128,128]{2,1,0:T(8,128)S(1)}, f32[16]{0:T(128)S(1)}, f32[16,128,128]{2,1,0:T(8,128)}, s32[]{:T(128)}, /*index=5*/s32[]{:T(128)}) %tuple.56), condition=%wide.region_7.8_spmd.clone, body=%wide.region_6.7_spmd.clone.sunk | while | flops 1310723 | bytes 6291639 | solution.py:145
  34.9 1.4 fusion.105
  36.3 3.4 %collective-permute-start = (bf16[16,128,128]{2,1,0:T(8,128)(2,1)S(1)}, bf16[16,128,128]{2,1,0:T(8,128)(2,1)}, u32[]{:S(2)}, u32[]{:S(2)}) collective-permute-start(bf16[16,128,128]{2,1,0:T(8,128)(2,1)S(1)} %fusion.105), channel_id=1, source_target_pairs={{0,4},{4,8},{8,12},{12,16},{16,20},{20,24},{24,28},{1,5},{5,9},{9,... | collective-permute-start | bytes 1572872 | tf_op jit(solution)/shard_map/while/body/eval_jaxpr/ppermute | solution.py:13
  39.7 13.0 %collective-permute-done = bf16[16,128,128]{2,1,0:T(8,128)(2,1)} collective-permute-done((bf16[16,128,128]{2,1,0:T(8,128)(2,1)S(1)}, bf16[16,128,128]{2,1,0:T(8,128)(2,1)}, u32[]{:S(2)}, u32[]{:S(2)}) %collective-permute-start) | collective-permute-done | bytes 524320 | tf_op jit(solution)/shard_map/while/body/eval_jaxpr/ppermute | solution.py:13
  52.7 1.1 convert_element_type.138
  53.8 1.4 fusion.105
  55.2 1.9 %collective-permute-start = (bf16[16,128,128]{2,1,0:T(8,128)(2,1)S(1)}, bf16[16,128,128]{2,1,0:T(8,128)(2,1)}, u32[]{:S(2)}, u32[]{:S(2)}) collective-permute-start(bf16[16,128,128]{2,1,0:T(8,128)(2,1)S(1)} %fusion.105), channel_id=1, source_target_pairs={{0,4},{4,8},{8,12},{12,16},{16,20},{20,24},{24,28},{1,5},{5,9},{9,... | collective-permute-start | bytes 1572872 | tf_op jit(solution)/shard_map/while/body/eval_jaxpr/ppermute | solution.py:13
  57.2 12.9 %collective-permute-done = bf16[16,128,128]{2,1,0:T(8,128)(2,1)} collective-permute-done((bf16[16,128,128]{2,1,0:T(8,128)(2,1)S(1)}, bf16[16,128,128]{2,1,0:T(8,128)(2,1)}, u32[]{:S(2)}, u32[]{:S(2)}) %collective-permute-start) | collective-permute-done | bytes 524320 | tf_op jit(solution)/shard_map/while/body/eval_jaxpr/ppermute | solution.py:13
  70.0 1.1 convert_element_type.138
  71.2 0.0 copy-start.3
  71.2 5.7 %fusion.33 = f32[16,128,384]{2,1,0:T(8,128)} fusion(f32[16,128,128]{2,1,0:T(8,128)S(1)} %get-tuple-element.24, f32[384,16]{0,1:T(8,128)S(1)} %get-tuple-element.80, bf16[384,2048]{1,0:T(8,128)(2,1)S(1)} %copy-done), kind=kOutput, calls=%fused_computation.43 | convolution fusion | flops 1209532416 | bytes 5791744 | tf_op jit(solution)/shard_map/thd,hde->the/dot_general | solution.py:146
  76.9 7.4 %multiply_reduce_fusion = (f32[384]{0:T(512)S(1)}, f32[384,16,128]{0,2,1:T(8,128)}) fusion(f32[384]{0:T(512)S(1)} %get-tuple-element.73, f32[16,128,384]{2,1,0:T(8,128)} %fusion.33, f32[16,384]{1,0:T(8,128)S(1)} %get-tuple-element.78, pred[384,384]{1,0:T(8,128)(4,1)S(1)} %copy-done.3, bf16[384,16,128]{0,2,1:T(8,128)(2,1)} %bitcast.214, ...), kind=kOutput, calls=%fused_computation.42 | convolution fusion | flops 1222901376 | bytes 11185152 | tf_op jit(solution)/shard_map/hts,shd->thd/dot_general | solution.py:40
  84.3 3.6 %copy.84 = f32[384,2048]{1,0:T(8,128)} copy(f32[384,2048]{0,1:T(8,128)} %bitcast.215) | data formatting | bytes 6291456 | tf_op jit(solution)/shard_map/reshape | solution.py:153
  87.9 5.8 %psum.7 = f32[384]{0:T(512)S(1)} all-reduce(f32[384]{0:T(512)S(1)} %get-tuple-element.87), channel_id=1, replica_groups=mesh['ctx'=8,'head'=4] {'head'}, use_global_device_ids=true, to_apply=%region_9.10 | all-reduce | flops 384 | bytes 3072 | tf_op jit(solution)/shard_map/psum | solution.py:154
  93.8 4.6 %multiply_convert_fusion.2 = bf16[384,2048]{1,0:T(8,128)(2,1)} fusion(bf16[384,2048]{1,0:T(8,128)(2,1)} %param.16, f32[384,2048]{1,0:T(8,128)} %copy.84, f32[2048]{0:T(1024)S(1)} %copy-done.5, f32[384]{0:T(512)S(1)} %add_rsqrt_fusion), kind=kLoop, calls=%fused_computation.41 | loop fusion | flops 6291456 | bytes 6301184 | tf_op jit(solution)/shard_map/convert_element_type | solution.py:161
  98.3 0.0 copy-done.1
  98.3 5.7 %fusion.2 = (f32[2,8,384]{2,1,0:T(8,128)S(1)}, f32[2,384,384,8]{2,1,3,0:T(8,128)}) fusion(pred[384,384]{0,1:T(8,128)(4,1)S(1)} %copy.85, bf16[384,2,128,1]{0,2,3,1:T(8,128)(2,1)S(1)} %bitcast.217, bf16[384,2,8,128]{3,2,1,0:T(8,128)(2,1)S(1)} %bitcast.210), kind=kOutput, calls=%fused_computation.10 | convolution fusion | flops 611051520 | bytes 11378688 | tf_op jit(solution)/shard_map/qkgd,skd->kgqs/dot_general | solution.py:68
  104.1 1.2 copy.95
  105.2 1.8 %copy.91 = pred[384,384]{0,1:T(8,128)(4,1)} copy(pred[384,384]{1,0:T(8,128)(4,1)} %get-tuple-element.83) | data formatting | bytes 294912 | tf_op jit(solution)/shard_map/and | solution.py:71
  107.1 0.0 collective-permute-done.3
  107.1 3.0 %fusion.4 = (f32[2,8,384]{2,1,0:T(8,128)S(1)}, f32[2,384,384,8]{2,1,3,0:T(8,128)S(1)}) fusion(pred[384,384]{0,1:T(8,128)(4,1)S(1)} %copy.95, bf16[384,2,8,128]{3,2,1,0:T(8,128)(2,1)S(1)} %bitcast.211, bf16[384,2,128]{2,0,1:T(8,128)(2,1)} %collective-permute-done.3), kind=kOutput, calls=%fused_computation.12 | convolution fusion | flops 611051520 | bytes 11378688 | tf_op jit(solution)/shard_map/qkgd,skd->kgqs/dot_general | solution.py:68
  110.1 0.0 collective-permute-done.1
  110.1 6.6 %fusion.3 = (f32[2,8,384]{2,1,0:T(8,128)S(1)}, f32[2,384,384,8]{2,1,3,0:T(8,128)}) fusion(pred[384,384]{0,1:T(8,128)(4,1)S(1)} %copy-done.2, bf16[384,2,8,128]{3,2,1,0:T(8,128)(2,1)S(1)} %bitcast.212, bf16[384,2,128]{2,0,1:T(8,128)(2,1)} %collective-permute-done.1), kind=kOutput, calls=%fused_computation.11 | convolution fusion | flops 611051520 | bytes 11378688 | tf_op jit(solution)/shard_map/qkgd,skd->kgqs/dot_general | solution.py:68
  116.7 0.0 slice-start
  116.7 0.0 slice-start.1
  116.7 6.1 %fusion.7 = f32[2,8,384]{2,1,0:T(8,128)S(1)} fusion(f32[2,384,384,8]{2,1,3,0:T(8,128)} %get-tuple-element.92, f32[2,8,384]{2,1,0:T(8,128)S(1)} %get-tuple-element.72, pred[384,384]{0,1:T(8,128)(4,1)S(1)} %copy-done.2), kind=kLoop, calls=%fused_computation.15 | loop fusion | flops 11790336 | bytes 9633792 | tf_op jit(solution)/shard_map/reduce_sum | solution.py:79
  122.9 0.0 slice-start.2
  122.9 2.5 %fusion.9 = f32[2,8,384]{2,1,0:T(8,128)S(1)} fusion(f32[2,384,384,8]{2,1,3,0:T(8,128)S(1)} %get-tuple-element.90, f32[2,8,384]{2,1,0:T(8,128)S(1)} %get-tuple-element.71, pred[384,384]{0,1:T(8,128)(4,1)S(1)} %copy.95), kind=kLoop, calls=%fused_computation.17 | loop fusion | flops 11790336 | bytes 9633792 | tf_op jit(solution)/shard_map/reduce_sum | solution.py:79
  125.4 2.3 %fusion.5 = f32[2,8,384]{2,1,0:T(8,128)S(1)} fusion(f32[2,384,384,8]{2,1,3,0:T(8,128)S(1)} %bitcast.209, f32[2,8,384]{2,1,0:T(8,128)S(1)} %get-tuple-element.77, pred[384,384]{0,1:T(8,128)(4,1)S(1)} %copy.85), kind=kLoop, calls=%fused_computation.13 | loop fusion | flops 11790336 | bytes 9633792 | tf_op jit(solution)/shard_map/reduce_sum | solution.py:79
  127.7 3.6 %fusion.19 = f32[2,8,384,128]{2,3,1,0:T(8,128)S(1)} fusion(bf16[384,2,128,1]{0,2,3,1:T(8,128)(2,1)} %bitcast.12, f32[2,384,384,8]{2,1,3,0:T(8,128)S(1)} %bitcast.209, f32[2,8,384]{2,1,0:T(8,128)S(1)} %get-tuple-element.77, pred[384,384]{0,1:T(8,128)(4,1)S(1)} %copy.85), kind=kOutput, calls=%fused_computation.25 | convolution fusion | flops 615776256 | bytes 12951552 | tf_op jit(solution)/shard_map/kgqs,skd->qkgd/dot_general | solution.py:80
  131.3 0.0 collective-permute-done.2
  131.3 5.4 %fusion.17 = f32[2,8,384,128]{2,3,1,0:T(8,128)S(1)} fusion(f32[2,384,384,8]{2,1,3,0:T(8,128)} %get-tuple-element.92, f32[2,8,384]{2,1,0:T(8,128)S(1)} %get-tuple-element.72, pred[384,384]{0,1:T(8,128)(4,1)S(1)} %copy-done.2, bf16[384,2,128]{0,2,1:T(8,128)(2,1)} %collective-permute-done.2), kind=kOutput, calls=%fused_computation.24 | convolution fusion | flops 615776256 | bytes 12951552 | tf_op jit(solution)/shard_map/kgqs,skd->qkgd/dot_general | solution.py:80
  136.8 0.0 collective-permute-done.4
  136.8 4.4 %fusion.29 = bf16[384,2,8,128]{0,3,2,1:T(8,128)(2,1)S(1)} fusion(f32[2,8,384,128]{2,3,1,0:T(8,128)S(1)} %fusion.17, f32[2,8,384,128]{2,3,1,0:T(8,128)S(1)} %fusion.19, f32[2,384,384,8]{2,1,3,0:T(8,128)S(1)} %get-tuple-element.90, f32[2,8,384]{2,1,0:T(8,128)S(1)} %get-tuple-element.71, pred[384,384]{0,1:T(8,128)(4,1)S(1)} %copy.95, ...), kind=kOutput, calls=%fused_computation.34 | convolution fusion | flops 622067712 | bytes 17769984 | tf_op jit(solution)/shard_map/kgqs,skd->qkgd/dot_general | solution.py:80
  141.2 1.6 %copy.99 = bf16[384,2048]{1,0:T(8,128)(2,1)} copy(bf16[384,2048]{0,1:T(8,128)(2,1)S(1)} %bitcast.219) | data formatting | bytes 3145728
  (26 shorter events, 0.2 us)
Async XLA Ops:
  0.6 70.6 %copy-start = (bf16[384,2048]{1,0:T(8,128)(2,1)S(1)}, bf16[384,2048]{1,0:T(8,128)(2,1)}, u32[]{:S(2)}) copy-start(bf16[384,2048]{1,0:T(8,128)(2,1)} %param.13) | copy-start | bytes 4718596
  0.6 23.1 %copy-start.6 = (s32[4]{0:T(128)S(1)}, s32[4]{0:T(128)}, u32[]{:S(2)}) copy-start(s32[4]{0:T(128)} %param.22) | copy-start | bytes 52
  0.7 23.1 %copy-start.7 = (s32[4]{0:T(128)S(1)}, s32[4]{0:T(128)}, u32[]{:S(2)}) copy-start(s32[4]{0:T(128)} %param.23) | copy-start | bytes 52
  0.7 25.5 %copy-start.4 = (f32[384,16]{0,1:T(8,128)S(1)}, f32[384,16]{0,1:T(8,128)}, u32[]{:S(2)}) copy-start(f32[384,16]{0,1:T(8,128)} %param.17) | copy-start | bytes 73732
  2.7 104.3 %collective-permute-start.3 = (bf16[384,2,128]{2,0,1:T(8,128)(2,1)}, bf16[384,2,128]{2,0,1:T(8,128)(2,1)}, u32[]{:S(2)}, u32[]{:S(2)}) collective-permute-start(bf16[384,2,128]{2,0,1:T(8,128)(2,1)} %copy.92), channel_id=1, source_target_pairs={{0,8},{4,12},{8,16},{12,20},{16,24},{20,28},{1,9},{5,13},{9,17},{1... | collective-permute-start | bytes 589832 | tf_op jit(solution)/shard_map/ppermute | solution.py:13
  6.2 103.9 %collective-permute-start.1 = (bf16[384,2,128]{2,0,1:T(8,128)(2,1)}, bf16[384,2,128]{2,0,1:T(8,128)(2,1)}, u32[]{:S(2)}, u32[]{:S(2)}) collective-permute-start(bf16[384,2,128]{2,0,1:T(8,128)(2,1)} %copy.92), channel_id=1, source_target_pairs={{0,4},{4,8},{8,12},{12,16},{16,20},{20,24},{24,28},{1,5},{5,9},{9,... | collective-permute-start | bytes 589832 | tf_op jit(solution)/shard_map/ppermute | solution.py:13
  11.4 120.0 %collective-permute-start.2 = (bf16[384,2,128]{0,2,1:T(8,128)(2,1)}, bf16[384,2,128]{0,2,1:T(8,128)(2,1)}, u32[]{:S(2)}, u32[]{:S(2)}) collective-permute-start(bf16[384,2,128]{0,2,1:T(8,128)(2,1)} %bitcast.10), channel_id=1, source_target_pairs={{0,4},{4,8},{8,12},{12,16},{16,20},{20,24},{24,28},{1,5},{5,9},{9,... | collective-permute-start | bytes 589832 | tf_op jit(solution)/shard_map/ppermute | solution.py:13
  14.8 122.0 %collective-permute-start.4 = (bf16[384,2,128]{0,2,1:T(8,128)(2,1)}, bf16[384,2,128]{0,2,1:T(8,128)(2,1)}, u32[]{:S(2)}, u32[]{:S(2)}) collective-permute-start(bf16[384,2,128]{0,2,1:T(8,128)(2,1)} %bitcast.10), channel_id=1, source_target_pairs={{0,8},{4,12},{8,16},{12,20},{16,24},{20,28},{1,9},{5,13},{9,17},{1... | collective-permute-start | bytes 589832 | tf_op jit(solution)/shard_map/ppermute | solution.py:13
  36.3 16.3 %collective-permute-start = (bf16[16,128,128]{2,1,0:T(8,128)(2,1)S(1)}, bf16[16,128,128]{2,1,0:T(8,128)(2,1)}, u32[]{:S(2)}, u32[]{:S(2)}) collective-permute-start(bf16[16,128,128]{2,1,0:T(8,128)(2,1)S(1)} %fusion.105), channel_id=1, source_target_pairs={{0,4},{4,8},{8,12},{12,16},{16,20},{20,24},{24,28},{1,5},{5,9},{9,... | collective-permute-start | bytes 1572872 | tf_op jit(solution)/shard_map/while/body/eval_jaxpr/ppermute | solution.py:13
  55.2 14.8 %collective-permute-start = (bf16[16,128,128]{2,1,0:T(8,128)(2,1)S(1)}, bf16[16,128,128]{2,1,0:T(8,128)(2,1)}, u32[]{:S(2)}, u32[]{:S(2)}) collective-permute-start(bf16[16,128,128]{2,1,0:T(8,128)(2,1)S(1)} %fusion.105), channel_id=1, source_target_pairs={{0,4},{4,8},{8,12},{12,16},{16,20},{20,24},{24,28},{1,5},{5,9},{9,... | collective-permute-start | bytes 1572872 | tf_op jit(solution)/shard_map/while/body/eval_jaxpr/ppermute | solution.py:13
  71.2 5.7 %copy-start.3 = (pred[384,384]{1,0:T(8,128)(4,1)S(1)}, pred[384,384]{1,0:T(8,128)(4,1)}, u32[]{:S(2)}) copy-start(pred[384,384]{1,0:T(8,128)(4,1)} %get-tuple-element.85) | copy-start | bytes 442372
  84.3 9.4 %copy-start.5 = (f32[2048]{0:T(1024)S(1)}, f32[2048]{0:T(1024)}, u32[]{:S(2)}) copy-start(f32[2048]{0:T(1024)} %param.18) | copy-start | bytes 24580
  93.8 4.6 %copy-start.1 = (bf16[48,8,16,128]{3,2,1,0:T(8,128)(2,1)S(1)}, bf16[48,8,16,128]{3,2,1,0:T(8,128)(2,1)}, u32[]{:S(2)}) copy-start(bf16[48,8,16,128]{3,2,1,0:T(8,128)(2,1)} %copy.117) | copy-start | bytes 4718596
  107.1 3.0 %copy-start.2 = (pred[384,384]{0,1:T(8,128)(4,1)S(1)}, pred[384,384]{0,1:T(8,128)(4,1)}, u32[]{:S(2)}) copy-start(pred[384,384]{0,1:T(8,128)(4,1)} %copy.91) | copy-start | bytes 442372
  116.7 8.6 %slice-start = ((s8[9437184]{0:T(1024)(128)(4,1)}), s8[4194304]{0:T(1024)(128)(4,1)S(1)}, s32[]{:S(2)}) async-start(s8[9437184]{0:T(1024)(128)(4,1)} %bitcast.208), calls=%async_computation | async-start | bytes 8388608
  116.7 8.6 %slice-start.1 = ((s8[9437184]{0:T(1024)(128)(4,1)}), s8[4194304]{0:T(1024)(128)(4,1)S(1)}, s32[]{:S(2)}) async-start(s8[9437184]{0:T(1024)(128)(4,1)} %bitcast.208), calls=%async_computation.1 | async-start | bytes 8388608
  122.9 2.5 %slice-start.2 = ((s8[9437184]{0:T(1024)(128)(4,1)}), s8[1048576]{0:T(1024)(128)(4,1)S(1)}, s32[]{:S(2)}) async-start(s8[9437184]{0:T(1024)(128)(4,1)} %bitcast.208), calls=%async_computation.2 | async-start | bytes 2097152
where the time goes:
time: 144 us; the launch traced here: 143 us
  matrix products  46.5 us (32%)
  other arithmetic  25.9 us (18%)
  waiting for transfers between devices  25.8 us (18%)
  local copies, waits for them, and re-layouts  18.8 us (13%)
  starting transfers between devices  17.6 us (12%)
  blocking collectives  5.84 us (4%)
  between operations  2.32 us (2%)
    ppermute x6, waiting for transfers between devices, passed_along(): return lax.ppermute(block, axis, route)  25.8 us
    ppermute x6, starting transfers between devices, passed_along(): return lax.ppermute(block, axis, route)  17.6 us
    dot_general x3, matrix products, attend(): jnp.einsum('qkgd,skd->kgqs', query, keys, preferred_element_type=jnp.floa...  15.3 us
    dot_general x3, matrix products, attend(): jnp.einsum('kgqs,skd->qkgd', probs.astype(jnp.bfloat16), values, preferre...  13.4 us
    reduce_sum x3, other arithmetic, attend(): running_sum = running_sum * shrink + jnp.sum(probs, axis=3)  10.9 us
    unnamed x26, local copies, waits for them, and re-layouts  7.6 us
    dot_general x1, matrix products, lightning_local(): jnp.einsum('hts,shd->thd', weights, values, preferred_element_type=jnp.fl...  7.41 us
    psum x1, blocking collectives, per_device(): square_sum = lax.psum(jnp.sum(flat * flat, axis=1), 'head')  5.84 us
  transfers between devices with their start and end apart: 6, of which 2 were waited for; matrix products, arithmetic and copies ran while one was open for 58% of the time, Pallas kernels for 0%

commit v1 on v0

v1 whole, which is shorter than its diff:
```python
import functools

import jax
import jax.numpy as jnp
from jax import lax
from jax.experimental import pallas as pl
from jax.experimental.pallas import tpu as pltpu
from jax.sharding import PartitionSpec as P

neg_big = -1e30
norm_eps = 1e-06
MESH = pl.DeviceIdType.MESH
TILE = 128
PARTS = 4


def dot_rows(a, b):
    return lax.dot_general(a, b, (((1,), (1,)), ((), ())), preferred_element_type=jnp.float32)


def dot_plain(a, b):
    return jnp.dot(a, b, preferred_element_type=jnp.float32)


def kernel(
    ctx_size,
    head_size,
    lq_hbm,
    lk_hbm,
    lv_hbm,
    gate_hbm,
    decay_ref,
    gain_ref,
    sq_hbm,
    sk_hbm,
    sv_hbm,
    starts_ref,
    lengths_ref,
    lin_hbm,
    soft_hbm,
    lq,
    lk,
    lv,
    gate,
    sq,
    sk,
    sv,
    far_k,
    far_v,
    state_mine,
    state_far,
    total_mine,
    total_far,
    decay_pad,
    c_row,
    c_all,
    enter_all,
    end_all,
    valid_col,
    bias,
    lin,
    peak,
    total,
    acc,
    square_mine,
    square_far,
    lin_stage,
    soft_stage,
    in_sem,
    out_sem,
    kv_send,
    kv_recv,
    state_send,
    state_recv,
    square_send,
    square_recv,
):
    rows, features = lq.shape
    heads = features // TILE
    kv_count = sk.shape[1] // TILE
    group = heads // kv_count
    seqs = starts_ref.shape[0]
    window = ctx_size // seqs
    row_tiles = rows // TILE
    reach = min(window * rows // 8, rows // 2)
    head_rows = -(-reach // TILE) * TILE
    me = lax.axis_index("ctx")
    mine = lax.axis_index("head")
    place = lax.rem(me, window)
    first = me * rows
    opening = place == 0

    loads = [
        pltpu.make_async_copy(source, target, in_sem.at[i])
        for i, (source, target) in enumerate(
            ((lk_hbm, lk), (lv_hbm, lv), (lq_hbm, lq), (sk_hbm, sk), (sv_hbm, sv), (sq_hbm, sq), (gate_hbm, gate))
        )
    ]
    for load in loads:
        load.start()

    def receives(distance):
        return (opening & (me > 0)) | (place >= distance)

    def sends(distance):
        target = lax.rem(me + distance, window)
        return (me + distance < ctx_size) & ((target == 0) | (target >= distance))

    barrier = pltpu.get_barrier_semaphore()
    for distance in range(1, window + 1):

        @pl.when(receives(distance))
        def greet_source():
            pl.semaphore_signal(barrier, inc=1, device_id={"ctx": me - distance}, device_id_type=MESH)

        @pl.when(sends(distance))
        def greet_target():
            pl.semaphore_signal(barrier, inc=1, device_id={"ctx": me + distance}, device_id_type=MESH)

    for step in range(1, head_size):
        peer = lax.rem(mine + step, head_size)
        pl.semaphore_signal(barrier, inc=1, device_id={"head": peer}, device_id_type=MESH)

    def segment_of(pos):
        segment = jnp.full(pos.shape, -1, jnp.int32)
        for s in range(seqs):
            segment = segment + jnp.where(starts_ref[s] <= pos, 1, 0)
        stop = jnp.zeros(pos.shape, jnp.int32)
        for s in range(seqs):
            stop = jnp.where(segment == s, starts_ref[s] + lengths_ref[s], stop)
        return segment, (segment >= 0) & (pos < stop)

    def segment_at(pos):
        segment = jnp.int32(-1)
        for s in range(seqs):
            segment = segment + jnp.where(starts_ref[s] <= pos, 1, 0)
        return segment

    before = segment_at(first - 1)
    last = segment_at(first + rows - 1)
    row_pos = lax.broadcasted_iota(jnp.int32, (rows, TILE), 0) + first
    row_seg, row_valid = segment_of(row_pos)
    valid_col[...] = row_valid.astype(jnp.float32)

    def key_code(owner):
        pos = lax.broadcasted_iota(jnp.int32, (8, rows), 1) + owner * rows
        segment, valid = segment_of(pos)
        return jnp.where(valid, segment, -7)[0:1]

    query_seg = row_seg[:, 0:1]
    own_code = key_code(me)
    order = lax.broadcasted_iota(jnp.int32, (rows, rows), 1) <= lax.broadcasted_iota(
        jnp.int32, (rows, rows), 0
    )
    bias[0] = jnp.where(order & (query_seg == own_code), 0.0, neg_big)
    for distance in range(1, window + 1):
        bias[distance] = jnp.where(query_seg == key_code(me - distance), 0.0, neg_big)

    decay_pad[...] = jnp.zeros_like(decay_pad)
    decay_pad[:, 0:heads] = decay_ref[...]
    lower = jnp.where(order, 1.0, 0.0)
    cumulative = lax.dot_general(
        lower,
        decay_pad[...],
        (((1,), (0,)), ((), ())),
        precision=lax.Precision.HIGHEST,
        preferred_element_type=jnp.float32,
    )
    c_all[...] = cumulative
    by_head = cumulative.T
    c_row[...] = by_head
    enter_all[...] = jnp.where(row_seg == before, jnp.exp(cumulative), 0.0)
    end_all[...] = jnp.where(
        (row_seg == last) & row_valid, jnp.exp(cumulative[rows - 1 : rows] - cumulative), 0.0
    )
    whole = jnp.exp(by_head[0:heads, rows - 1 : rows]) * jnp.where(last == before, 1.0, 0.0)
    total_mine[...] = jnp.broadcast_to(whole, (heads, TILE))

    greetings = head_size - 1
    for distance in range(1, window + 1):
        greetings = greetings + jnp.where(receives(distance), 1, 0)
        greetings = greetings + jnp.where(sends(distance), 1, 0)
    pl.semaphore_wait(barrier, greetings)

    def total_copy(distance):
        return pltpu.make_async_remote_copy(
            src_ref=total_mine,
            dst_ref=total_far.at[distance - 1],
            send_sem=state_send.at[distance - 1, PARTS],
            recv_sem=state_recv.at[distance - 1, PARTS],
            device_id={"ctx": me + distance},
            device_id_type=MESH,
        )

    share = heads // PARTS

    def state_copy(distance, part):
        span = pl.ds(part * share, share)
        return pltpu.make_async_remote_copy(
            src_ref=state_mine.at[span],
            dst_ref=state_far.at[distance - 1, span],
            send_sem=state_send.at[distance - 1, part],
            recv_sem=state_recv.at[distance - 1, part],
            device_id={"ctx": me + distance},
            device_id_type=MESH,
        )

    def kv_copies(distance):
        return [
            pltpu.make_async_remote_copy(
                src_ref=source,
                dst_ref=target.at[distance - 1],
                send_sem=kv_send.at[distance - 1, i],
                recv_sem=kv_recv.at[distance - 1, i],
                device_id={"ctx": me + distance},
                device_id_type=MESH,
            )
            for i, (source, target) in enumerate(((sk_hbm, far_k), (sv_hbm, far_v)))
        ]

    def far_copies(distance):
        return (
            [total_copy(distance)]
            + [state_copy(distance, part) for part in range(PARTS)]
            + kv_copies(distance)
        )

    def lanes(head):
        return pl.ds(pl.multiple_of(head * TILE, TILE), TILE)

    lane_id = lax.broadcasted_iota(jnp.int32, (rows, TILE), 1)

    def column(ref, head):
        return jnp.sum(jnp.where(lane_id == head, ref[...], 0.0), axis=1, keepdims=True)

    loads[0].wait()
    loads[1].wait()

    def make_state(head, carry):
        scaled = (lk[:, lanes(head)].astype(jnp.float32) * column(end_all, head)).astype(jnp.bfloat16)
        local = lax.dot_general(
            scaled, lv[:, lanes(head)], (((0,), (0,)), ((), ())), preferred_element_type=jnp.float32
        )
        state_mine[head] = local.astype(jnp.bfloat16)
        return carry

    for part in range(PARTS):
        lax.fori_loop(part * share, (part + 1) * share, make_state, 0)
        for distance in range(1, window + 1):

            @pl.when(sends(distance))
            def send_state():
                if part == 0:
                    total_copy(distance).start()
                state_copy(distance, part).start()

    for distance in range(1, window + 1):

        @pl.when(sends(distance))
        def send_keys():
            for copy in kv_copies(distance):
                copy.start()

    for load in loads[2:6]:
        load.wait()
    score_scale = TILE ** (-0.5)

    def within(head, carry):
        c_col = column(c_all, head)
        c_line = c_row[pl.ds(head, 1), :]
        span = lanes(head)
        kv_span = lanes(head // group)
        for tile in range(row_tiles):
            at = slice(tile * TILE, (tile + 1) * TILE)
            wide = (tile + 1) * TILE
            hidden = bias[0, at, 0:wide]
            factor = jnp.exp(c_col[at] - c_line[:, 0:wide] + hidden)
            weights = (dot_rows(lq[at, span], lk[0:wide, span]) * factor).astype(jnp.bfloat16)
            lin[at, span] = dot_plain(weights, lv[0:wide, span])
            scores = dot_rows(sq[at, span], sk[0:wide, kv_span]) * score_scale + hidden
            top = jnp.max(scores, axis=1, keepdims=True)
            probs = jnp.exp(scores - top)
            peak[head, at, :] = jnp.broadcast_to(top, (TILE, TILE))
            total[head, at, :] = jnp.broadcast_to(jnp.sum(probs, axis=1, keepdims=True), (TILE, TILE))
            acc[at, span] = dot_plain(probs.astype(jnp.bfloat16), sv[0:wide, kv_span])
        return carry

    lax.fori_loop(0, heads, within, 0)

    for distance in range(1, window + 1):

        @pl.when(receives(distance))
        def await_state():
            total_copy(distance).wait_recv()
            for part in range(PARTS):
                state_copy(distance, part).wait_recv()

    def carried_over(count, distances):
        def body(head, carry):
            state = state_far[0, head].astype(jnp.float32)
            if distances > 1:
                scale = total_far[0, pl.ds(head, 1), :]
                for index in range(1, distances):
                    state = state + scale * state_far[index, head].astype(jnp.float32)
                    scale = scale * total_far[index, pl.ds(head, 1), :]
            enter = column(enter_all, head)[0:count]
            span = lanes(head)
            lin[0:count, span] += enter * dot_plain(lq[0:count, span], state.astype(jnp.bfloat16))
            return carry

        lax.fori_loop(0, heads, body, 0)

    @pl.when(opening & (me > 0))
    def carry_opening():
        carried_over(head_rows, window)

    for distance in range(1, window):

        @pl.when(place == distance)
        def carry_inside():
            carried_over(rows, distance)

    def square(head, so_far):
        value = lin[:, lanes(head)] * valid_col[...]
        return so_far + value * value

    squares = lax.fori_loop(0, heads, square, jnp.zeros((rows, TILE), jnp.float32))
    square_mine[...] = lax.dot_general(
        jnp.ones((8, TILE), jnp.float32),
        squares,
        (((1,), (1,)), ((), ())),
        precision=lax.Precision.HIGHEST,
        preferred_element_type=jnp.float32,
    )

    def square_copy(step):
        return pltpu.make_async_remote_copy(
            src_ref=square_mine,
            dst_ref=square_far.at[step - 1],
            send_sem=square_send.at[step - 1],
            recv_sem=square_recv.at[step - 1],
            device_id={"head": lax.rem(mine + step, head_size)},
            device_id_type=MESH,
        )

    for step in range(1, head_size):
        square_copy(step).start()

    for distance in range(1, window + 1):

        @pl.when(receives(distance))
        def await_keys():
            for copy in kv_copies(distance):
                copy.wait_recv()

    def attend_far(count, distances):
        def body(head, carry):
            span = lanes(head)
            kv_span = lanes(head // group)
            for tile in range(count // TILE):
                at = slice(tile * TILE, (tile + 1) * TILE)
                top = peak[head, at, :][:, 0:1]
                sums = total[head, at, :][:, 0:1]
                mixed = acc[at, span]
                query = sq[at, span]
                for index in range(distances):
                    scores = dot_rows(query, far_k[index, :, kv_span]) * score_scale
                    scores = scores + bias[index + 1, at, :]
                    higher = jnp.maximum(top, jnp.max(scores, axis=1, keepdims=True))
                    shrink = jnp.exp(top - higher)
                    probs = jnp.exp(scores - higher)
                    sums = sums * shrink + jnp.sum(probs, axis=1, keepdims=True)
                    mixed = mixed * shrink + dot_plain(
                        probs.astype(jnp.bfloat16), far_v[index, :, kv_span]
                    )
                    top = higher
                total[head, at, :] = jnp.broadcast_to(sums, (TILE, TILE))
                acc[at, span] = mixed
            return carry

        lax.fori_loop(0, heads, body, 0)

    @pl.when(opening & (me > 0))
    def attend_opening():
        attend_far(head_rows, window)

    for distance in range(1, window):

        @pl.when(place == distance)
        def attend_inside():
            attend_far(rows, distance)

    def finish_soft(head, carry):
        span = lanes(head)
        soft_stage[:, span] = (acc[:, span] / total[head] * valid_col[...]).astype(jnp.bfloat16)
        return carry

    lax.fori_loop(0, heads, finish_soft, 0)
    soft_store = pltpu.make_async_copy(soft_stage, soft_hbm, out_sem.at[0])
    soft_store.start()

    loads[6].wait()
    for step in range(1, head_size):
        square_copy(step).wait_recv()
    summed = square_mine[...]
    for step in range(1, head_size):
        summed = summed + square_far[step - 1]
    inverse = lax.rsqrt(summed * (1.0 / (features * head_size)) + norm_eps)
    enter_all[...] = jnp.broadcast_to(inverse[0:1], (TILE, rows)).T * valid_col[...]

    def finish_lin(head, carry):
        span = lanes(head)
        opened = jax.nn.sigmoid(gate[:, span].astype(jnp.float32))
        lin_stage[:, span] = (lin[:, span] * enter_all[...] * gain_ref[:, span] * opened).astype(
            jnp.bfloat16
        )
        return carry

    lax.fori_loop(0, heads, finish_lin, 0)
    lin_store = pltpu.make_async_copy(lin_stage, lin_hbm, out_sem.at[1])
    lin_store.start()
    for distance in range(1, window + 1):

        @pl.when(sends(distance))
        def drain():
            for copy in far_copies(distance):
                copy.wait_send()

    for step in range(1, head_size):
        square_copy(step).wait_send()
    soft_store.wait()
    lin_store.wait()


def per_device(
    lin_query,
    lin_key,
    lin_value,
    lin_gate,
    lin_decay,
    norm_gain,
    soft_query,
    soft_key,
    soft_value,
    starts,
    lengths,
):
    rows, features = lin_query.shape
    kv_features = soft_key.shape[1]
    heads = features // TILE
    ctx_size, head_size = lax.axis_size("ctx"), lax.axis_size("head")
    window = ctx_size // starts.shape[0]
    f32, bf16 = jnp.float32, jnp.bfloat16
    anywhere = pl.BlockSpec(memory_space=pl.ANY)
    vmem = pl.BlockSpec(memory_space=pltpu.VMEM)
    smem = pl.BlockSpec(memory_space=pltpu.SMEM)
    wide = pltpu.VMEM((rows, features), bf16)
    narrow = pltpu.VMEM((rows, kv_features), bf16)
    dma = pltpu.SemaphoreType.DMA
    scratch = [wide, wide, wide, wide, wide, narrow, narrow]
    scratch += [
        pltpu.VMEM((window, rows, kv_features), bf16),
        pltpu.VMEM((window, rows, kv_features), bf16),
        pltpu.VMEM((heads, TILE, TILE), bf16),
        pltpu.VMEM((window, heads, TILE, TILE), bf16),
        pltpu.VMEM((heads, TILE), f32),
        pltpu.VMEM((window, heads, TILE), f32),
        pltpu.VMEM((rows, TILE), f32),
        pltpu.VMEM((TILE, rows), f32),
        pltpu.VMEM((rows, TILE), f32),
        pltpu.VMEM((rows, TILE), f32),
        pltpu.VMEM((rows, TILE), f32),
        pltpu.VMEM((rows, TILE), f32),
        pltpu.VMEM((window + 1, rows, rows), f32),
        pltpu.VMEM((rows, features), f32),
        pltpu.VMEM((heads, rows, TILE), f32),
        pltpu.VMEM((heads, rows, TILE), f32),
        pltpu.VMEM((rows, features), f32),
        pltpu.VMEM((8, rows), f32),
        pltpu.VMEM((head_size - 1, 8, rows), f32),
        wide,
        wide,
        dma((7,)),
        dma((2,)),
        dma((window, 2)),
        dma((window, 2)),
        dma((window, PARTS + 1)),
        dma((window, PARTS + 1)),
        dma((head_size - 1,)),
        dma((head_size - 1,)),
    ]
    out = jax.ShapeDtypeStruct((rows, features), bf16)
    return pl.pallas_call(
        functools.partial(kernel, ctx_size, head_size),
        out_shape=(out, out),
        in_specs=[anywhere] * 4 + [vmem, vmem] + [anywhere] * 3 + [smem, smem],
        out_specs=(anywhere, anywhere),
        scratch_shapes=scratch,
        compiler_params=pltpu.CompilerParams(
            collective_id=0, has_side_effects=True, vmem_limit_bytes=56 * 1024 * 1024
        ),
    )(
        lin_query,
        lin_key,
        lin_value,
        lin_gate,
        lin_decay,
        norm_gain.reshape(1, features),
        soft_query,
        soft_key,
        soft_value,
        starts,
        lengths,
    )


def solution(mesh):
    both = P("ctx", "head")
    placed = (both, both, both, both, both, P("head"), both, both, both, P(), P())
    return jax.shard_map(
        per_device, mesh=mesh, in_specs=placed, out_specs=(both, both), check_vma=False
    )
```

time: 144 us -> 62.3 us (0.43)
  the two profiles are of different devices: /device:TPU:12 before, /device:TPU:18 now
where the time goes in v1:
time: 62.3 us; the launch traced here: 62.1 us
  Pallas kernels  55.9 us (90%)
  local copies, waits for them, and re-layouts  5.54 us (9%)
  between operations  0.65 us (1%)
    pallas_call x1, Pallas kernels, per_device(): pl.pallas_call(functools.partial(kernel, ctx_size, head_size), out_shape=...  55.9 us
    unnamed x5, local copies, waits for them, and re-layouts  5.54 us

profile of v1, /device:TPU:18, one launch (start us, length us, event | category | flops | bytes accessed | tf_op | source)
XLA Modules:
  0.0 62.1 jit_solution(16884147254976750969)
XLA Ops:
  0.6 1.5 %copy.13.decay_ref = f32[384,16]{1,0:T(8,128)} copy(f32[384,16]{0,1:T(8,128)} %param.15) | data formatting | bytes 49152 | tf_op args[4]
  2.2 55.9 %shard_map.122 = (bf16[384,2048]{1,0:T(8,128)(2,1)}, bf16[384,2048]{1,0:T(8,128)(2,1)}) custom-call(bf16[384,2048]{1,0:T(8,128)(2,1)} %lq_hbm.1, bf16[384,2048]{1,0:T(8,128)(2,1)} %lk_hbm.1, bf16[384,2048]{1,0:T(8,128)(2,1)} %lv_hbm.1, bf16[384,2048]{1,0:T(8,128)(2,1)} %gate_hbm.1, f32[384,16]{1,0:T(8,128)} %copy.13.decay_ref, f32[1,2048]{1,0:T(1,128)} %bitcast.1, ...), custom_call_target="tpu_custom_call" | custom-call | tf_op jit(solution)/shard_map/pallas_call | solution.py:493
  58.1 0.0 copy-start
  58.1 2.8 %copy.16 = bf16[384,2048]{1,0:T(8,128)(2,1)} copy(bf16[384,2048]{1,0:T(8,128)(2,1)} %get-tuple-element.4) | data formatting | bytes 3145728
  60.9 0.0 copy-done
  60.9 1.1 %copy.17 = bf16[384,2048]{1,0:T(8,128)(2,1)} copy(bf16[384,2048]{1,0:T(8,128)(2,1)S(1)} %copy-done) | data formatting | bytes 3145728
Async XLA Ops:
  58.1 2.9 %copy-start = (bf16[384,2048]{1,0:T(8,128)(2,1)S(1)}, bf16[384,2048]{1,0:T(8,128)(2,1)}, u32[]{:S(2)}) copy-start(bf16[384,2048]{1,0:T(8,128)(2,1)} %get-tuple-element.5) | copy-start | bytes 4718596

commit v2 on v1

--- a/solution.py
+++ b/solution.py
@@ -12,6 +12,7 @@
 MESH = pl.DeviceIdType.MESH
 TILE = 128
 PARTS = 4
+log2_e = 1.4426950408889634
 
 
 def dot_rows(a, b):
@@ -51,7 +52,6 @@
     state_far,
     total_mine,
     total_far,
-    decay_pad,
     c_row,
     c_all,
     enter_all,
@@ -59,9 +59,6 @@
     valid_col,
     bias,
     lin,
-    peak,
-    total,
-    acc,
     square_mine,
     square_far,
     lin_stage,
@@ -156,24 +153,28 @@
     for distance in range(1, window + 1):
         bias[distance] = jnp.where(query_seg == key_code(me - distance), 0.0, neg_big)
 
-    decay_pad[...] = jnp.zeros_like(decay_pad)
-    decay_pad[:, 0:heads] = decay_ref[...]
-    lower = jnp.where(order, 1.0, 0.0)
-    cumulative = lax.dot_general(
-        lower,
-        decay_pad[...],
+    upper = jnp.where(
+        lax.broadcasted_iota(jnp.int32, (rows, rows), 0)
+        <= lax.broadcasted_iota(jnp.int32, (rows, rows), 1),
+        log2_e,
+        0.0,
+    )
+    c_row[...] = jnp.zeros_like(c_row)
+    c_row[0:heads, :] = lax.dot_general(
+        decay_ref[...],
+        upper,
         (((1,), (0,)), ((), ())),
         precision=lax.Precision.HIGHEST,
         preferred_element_type=jnp.float32,
     )
+    by_head = c_row[...]
+    cumulative = by_head.T
     c_all[...] = cumulative
-    by_head = cumulative.T
-    c_row[...] = by_head
-    enter_all[...] = jnp.where(row_seg == before, jnp.exp(cumulative), 0.0)
+    enter_all[...] = jnp.where(row_seg == before, jnp.exp2(cumulative), 0.0)
     end_all[...] = jnp.where(
-        (row_seg == last) & row_valid, jnp.exp(cumulative[rows - 1 : rows] - cumulative), 0.0
-    )
-    whole = jnp.exp(by_head[0:heads, rows - 1 : rows]) * jnp.where(last == before, 1.0, 0.0)
+        (row_seg == last) & row_valid, jnp.exp2(cumulative[rows - 1 : rows] - cumulative), 0.0
+    )
+    whole = jnp.exp2(by_head[0:heads, rows - 1 : rows]) * jnp.where(last == before, 1.0, 0.0)
     total_mine[...] = jnp.broadcast_to(whole, (heads, TILE))
 
     greetings = head_size - 1
@@ -233,19 +234,27 @@
     def column(ref, head):
         return jnp.sum(jnp.where(lane_id == head, ref[...], 0.0), axis=1, keepdims=True)
 
+    for distance in range(1, window + 1):
+
+        @pl.when(sends(distance))
+        def send_keys():
+            for copy in kv_copies(distance):
+                copy.start()
+
     loads[0].wait()
     loads[1].wait()
 
-    def make_state(head, carry):
+    def make_state(head):
         scaled = (lk[:, lanes(head)].astype(jnp.float32) * column(end_all, head)).astype(jnp.bfloat16)
         local = lax.dot_general(
             scaled, lv[:, lanes(head)], (((0,), (0,)), ((), ())), preferred_element_type=jnp.float32
         )
-        state_mine[head] = local.astype(jnp.bfloat16)
-        return carry
+        return local.astype(jnp.bfloat16)
 
     for part in range(PARTS):
-        lax.fori_loop(part * share, (part + 1) * share, make_state, 0)
+        made = [make_state(head) for head in range(part * share, (part + 1) * share)]
+        for index, local in enumerate(made):
+            state_mine[part * share + index] = local
         for distance in range(1, window + 1):
 
             @pl.when(sends(distance))
@@ -254,38 +263,91 @@
                     total_copy(distance).start()
                 state_copy(distance, part).start()
 
-    for distance in range(1, window + 1):
-
-        @pl.when(sends(distance))
-        def send_keys():
+    loads[2].wait()
+
+    def within(pair, carry):
+        made = []
+        for head in (2 * pair, 2 * pair + 1):
+            c_col = column(c_all, head)
+            c_line = c_row[pl.ds(head, 1), :]
+            span = lanes(head)
+            for tile in range(row_tiles):
+                at = slice(tile * TILE, (tile + 1) * TILE)
+                wide = (tile + 1) * TILE
+                factor = jnp.exp2(c_col[at] - c_line[:, 0:wide] + bias[0, at, 0:wide])
+                weights = (dot_rows(lq[at, span], lk[0:wide, span]) * factor).astype(jnp.bfloat16)
+                made.append((at, span, dot_plain(weights, lv[0:wide, span])))
+        for at, span, value in made:
+            lin[at, span] = value
+        return carry
+
+    lax.fori_loop(0, heads // 2, within, 0)
+
+    for load in loads[3:6]:
+        load.wait()
+    for distance in range(1, window + 1):
+
+        @pl.when(receives(distance))
+        def await_keys():
             for copy in kv_copies(distance):
-                copy.start()
-
-    for load in loads[2:6]:
-        load.wait()
-    score_scale = TILE ** (-0.5)
-
-    def within(head, carry):
-        c_col = column(c_all, head)
-        c_line = c_row[pl.ds(head, 1), :]
-        span = lanes(head)
-        kv_span = lanes(head // group)
-        for tile in range(row_tiles):
-            at = slice(tile * TILE, (tile + 1) * TILE)
-            wide = (tile + 1) * TILE
-            hidden = bias[0, at, 0:wide]
-            factor = jnp.exp(c_col[at] - c_line[:, 0:wide] + hidden)
-            weights = (dot_rows(lq[at, span], lk[0:wide, span]) * factor).astype(jnp.bfloat16)
-            lin[at, span] = dot_plain(weights, lv[0:wide, span])
-            scores = dot_rows(sq[at, span], sk[0:wide, kv_span]) * score_scale + hidden
-            top = jnp.max(scores, axis=1, keepdims=True)
-            probs = jnp.exp(scores - top)
-            peak[head, at, :] = jnp.broadcast_to(top, (TILE, TILE))
-            total[head, at, :] = jnp.broadcast_to(jnp.sum(probs, axis=1, keepdims=True), (TILE, TILE))
-            acc[at, span] = dot_plain(probs.astype(jnp.bfloat16), sv[0:wide, kv_span])
-        return carry
-
-    lax.fori_loop(0, heads, within, 0)
+                copy.wait_recv()
+
+    score_scale = log2_e * TILE ** (-0.5)
+    ones = jnp.ones((rows, TILE), jnp.bfloat16)
+
+    def attend_all(pairs_from, pairs_to, far_rows, distances):
+        def body(pair, carry):
+            made = []
+            for head in (2 * pair, 2 * pair + 1):
+                span = lanes(head)
+                kv_span = lanes(head // group)
+                for tile in range(row_tiles):
+                    at = slice(tile * TILE, (tile + 1) * TILE)
+                    wide = (tile + 1) * TILE
+                    query = sq[at, span]
+                    pieces = [
+                        (
+                            dot_rows(query, sk[0:wide, kv_span]) * score_scale + bias[0, at, 0:wide],
+                            sv[0:wide, kv_span],
+                        )
+                    ]
+                    if tile * TILE < far_rows:
+                        for index in range(distances):
+                            scores = dot_rows(query, far_k[index, :, kv_span]) * score_scale
+                            pieces.append((scores + bias[index + 1, at, :], far_v[index, :, kv_span]))
+                    top = jnp.max(pieces[0][0], axis=1, keepdims=True)
+                    for scores, value in pieces[1:]:
+                        top = jnp.maximum(top, jnp.max(scores, axis=1, keepdims=True))
+                    mixed = None
+                    for scores, value in pieces:
+                        probs = jnp.exp2(scores - top).astype(jnp.bfloat16)
+                        both = jnp.concatenate([value, ones[0 : value.shape[0]]], axis=1)
+                        term = dot_plain(probs, both)
+                        mixed = term if mixed is None else mixed + term
+                    result = mixed[:, 0:TILE] * (valid_col[at, :] / mixed[:, TILE:])
+                    made.append((at, span, result.astype(jnp.bfloat16)))
+            for at, span, value in made:
+                soft_stage[at, span] = value
+            return carry
+
+        lax.fori_loop(pairs_from, pairs_to, body, 0)
+
+    def attend(pairs_from, pairs_to):
+        @pl.when(me == 0)
+        def attend_own():
+            attend_all(pairs_from, pairs_to, 0, 0)
+
+        @pl.when(opening & (me > 0))
+        def attend_opening():
+            attend_all(pairs_from, pairs_to, head_rows, window)
+
+        for distance in range(1, window):
+
+            @pl.when(place == distance)
+            def attend_inside():
+                attend_all(pairs_from, pairs_to, rows, distance)
+
+    attend(0, heads // 4)
 
     for distance in range(1, window + 1):
 
@@ -346,56 +408,7 @@
     for step in range(1, head_size):
         square_copy(step).start()
 
-    for distance in range(1, window + 1):
-
-        @pl.when(receives(distance))
-        def await_keys():
-            for copy in kv_copies(distance):
-                copy.wait_recv()
-
-    def attend_far(count, distances):
-        def body(head, carry):
-            span = lanes(head)
-            kv_span = lanes(head // group)
-            for tile in range(count // TILE):
-                at = slice(tile * TILE, (tile + 1) * TILE)
-                top = peak[head, at, :][:, 0:1]
-                sums = total[head, at, :][:, 0:1]
-                mixed = acc[at, span]
-                query = sq[at, span]
-                for index in range(distances):
-                    scores = dot_rows(query, far_k[index, :, kv_span]) * score_scale
-                    scores = scores + bias[index + 1, at, :]
-                    higher = jnp.maximum(top, jnp.max(scores, axis=1, keepdims=True))
-                    shrink = jnp.exp(top - higher)
-                    probs = jnp.exp(scores - higher)
-                    sums = sums * shrink + jnp.sum(probs, axis=1, keepdims=True)
-                    mixed = mixed * shrink + dot_plain(
-                        probs.astype(jnp.bfloat16), far_v[index, :, kv_span]
-                    )
-                    top = higher
-                total[head, at, :] = jnp.broadcast_to(sums, (TILE, TILE))
-                acc[at, span] = mixed
-            return carry
-
-        lax.fori_loop(0, heads, body, 0)
-
-    @pl.when(opening & (me > 0))
-    def attend_opening():
-        attend_far(head_rows, window)
-
-    for distance in range(1, window):
-
-        @pl.when(place == distance)
-        def attend_inside():
-            attend_far(rows, distance)
-
-    def finish_soft(head, carry):
-        span = lanes(head)
-        soft_stage[:, span] = (acc[:, span] / total[head] * valid_col[...]).astype(jnp.bfloat16)
-        return carry
-
-    lax.fori_loop(0, heads, finish_soft, 0)
+    attend(heads // 4, heads // 2)
     soft_store = pltpu.make_async_copy(soft_stage, soft_hbm, out_sem.at[0])
     soft_store.start()
 
@@ -410,7 +423,7 @@
 
     def finish_lin(head, carry):
         span = lanes(head)
-        opened = jax.nn.sigmoid(gate[:, span].astype(jnp.float32))
+        opened = 0.5 + 0.5 * jnp.tanh(0.5 * gate[:, span].astype(jnp.float32))
         lin_stage[:, span] = (lin[:, span] * enter_all[...] * gain_ref[:, span] * opened).astype(
             jnp.bfloat16
         )
@@ -465,16 +478,12 @@
         pltpu.VMEM((window, heads, TILE, TILE), bf16),
         pltpu.VMEM((heads, TILE), f32),
         pltpu.VMEM((window, heads, TILE), f32),
-        pltpu.VMEM((rows, TILE), f32),
         pltpu.VMEM((TILE, rows), f32),
         pltpu.VMEM((rows, TILE), f32),
         pltpu.VMEM((rows, TILE), f32),
         pltpu.VMEM((rows, TILE), f32),
         pltpu.VMEM((rows, TILE), f32),
         pltpu.VMEM((window + 1, rows, rows), f32),
-        pltpu.VMEM((rows, features), f32),
-        pltpu.VMEM((heads, rows, TILE), f32),
-        pltpu.VMEM((heads, rows, TILE), f32),
         pltpu.VMEM((rows, features), f32),
         pltpu.VMEM((8, rows), f32),
         pltpu.VMEM((head_size - 1, 8, rows), f32),
@@ -504,7 +513,7 @@
         lin_key,
         lin_value,
         lin_gate,
-        lin_decay,
+        lin_decay.T,
         norm_gain.reshape(1, features),
         soft_query,
         soft_key,

time: 62.3 us -> 43 us (0.69)
  Pallas kernels: 55.9 us -> 38.2 us
  local copies, waits for them, and re-layouts: 5.54 us -> 3.99 us
    pallas_call x1, Pallas kernels: 55.9 us -> 38.2 us  [per_device(): pl.pallas_call(functools.partial(kernel, ctx_size, head_size), out_shape=...]
    unnamed x5 -> x4, local copies, waits for them, and re-layouts: 5.54 us -> 3.99 us
where the time goes in v2:
time: 43 us; the launch traced here: 42.8 us
  Pallas kernels  38.2 us (89%)
  local copies, waits for them, and re-layouts  3.99 us (9%)
  between operations  0.65 us (2%)
    pallas_call x1, Pallas kernels, per_device(): pl.pallas_call(functools.partial(kernel, ctx_size, head_size), out_shape=...  38.2 us
    unnamed x4, local copies, waits for them, and re-layouts  3.99 us

profile of v2, /device:TPU:18, one launch (start us, length us, event | category | flops | bytes accessed | tf_op | source)
XLA Modules:
  0.0 42.8 jit_solution(3332448306976515015)
XLA Ops:
  0.6 38.2 %shard_map.122 = (bf16[384,2048]{1,0:T(8,128)(2,1)}, bf16[384,2048]{1,0:T(8,128)(2,1)}) custom-call(bf16[384,2048]{1,0:T(8,128)(2,1)} %lq_hbm.1, bf16[384,2048]{1,0:T(8,128)(2,1)} %lk_hbm.1, bf16[384,2048]{1,0:T(8,128)(2,1)} %lv_hbm.1, bf16[384,2048]{1,0:T(8,128)(2,1)} %gate_hbm.1, f32[16,384]{1,0:T(8,128)} %bitcast.2, f32[1,2048]{1,0:T(1,128)} %bitcast.3, ...), custom_call_target="tpu_custom_call" | custom-call | tf_op jit(solution)/shard_map/pallas_call | solution.py:502
  38.8 0.0 copy-start
  38.8 2.8 %copy.15 = bf16[384,2048]{1,0:T(8,128)(2,1)} copy(bf16[384,2048]{1,0:T(8,128)(2,1)} %get-tuple-element.4) | data formatting | bytes 3145728
  41.6 0.0 copy-done
  41.7 1.1 %copy.16 = bf16[384,2048]{1,0:T(8,128)(2,1)} copy(bf16[384,2048]{1,0:T(8,128)(2,1)S(1)} %copy-done) | data formatting | bytes 3145728
Async XLA Ops:
  38.8 2.9 %copy-start = (bf16[384,2048]{1,0:T(8,128)(2,1)S(1)}, bf16[384,2048]{1,0:T(8,128)(2,1)}, u32[]{:S(2)}) copy-start(bf16[384,2048]{1,0:T(8,128)(2,1)} %get-tuple-element.5) | copy-start | bytes 4718596

commit v3 on v2

--- a/solution.py
+++ b/solution.py
@@ -265,9 +265,9 @@
 
     loads[2].wait()
 
-    def within(pair, carry):
+    def within(quad, carry):
         made = []
-        for head in (2 * pair, 2 * pair + 1):
+        for head in [4 * quad + i for i in range(4)]:
             c_col = column(c_all, head)
             c_line = c_row[pl.ds(head, 1), :]
             span = lanes(head)
@@ -281,7 +281,7 @@
             lin[at, span] = value
         return carry
 
-    lax.fori_loop(0, heads // 2, within, 0)
+    lax.fori_loop(0, heads // 4, within, 0)
 
     for load in loads[3:6]:
         load.wait()
@@ -358,19 +358,25 @@
                 state_copy(distance, part).wait_recv()
 
     def carried_over(count, distances):
-        def body(head, carry):
-            state = state_far[0, head].astype(jnp.float32)
-            if distances > 1:
-                scale = total_far[0, pl.ds(head, 1), :]
-                for index in range(1, distances):
-                    state = state + scale * state_far[index, head].astype(jnp.float32)
-                    scale = scale * total_far[index, pl.ds(head, 1), :]
-            enter = column(enter_all, head)[0:count]
-            span = lanes(head)
-            lin[0:count, span] += enter * dot_plain(lq[0:count, span], state.astype(jnp.bfloat16))
+        def body(quad, carry):
+            made = []
+            for head in [4 * quad + i for i in range(4)]:
+                state = state_far[0, head]
+                if distances > 1:
+                    state = state.astype(jnp.float32)
+                    scale = total_far[0, pl.ds(head, 1), :]
+                    for index in range(1, distances):
+                        state = state + scale * state_far[index, head].astype(jnp.float32)
+                        scale = scale * total_far[index, pl.ds(head, 1), :]
+                    state = state.astype(jnp.bfloat16)
+                enter = column(enter_all, head)[0:count]
+                span = lanes(head)
+                made.append((span, lin[0:count, span] + enter * dot_plain(lq[0:count, span], state)))
+            for span, value in made:
+                lin[0:count, span] = value
             return carry
 
-        lax.fori_loop(0, heads, body, 0)
+        lax.fori_loop(0, heads // 4, body, 0)
 
     @pl.when(opening & (me > 0))
     def carry_opening():
@@ -382,11 +388,14 @@
         def carry_inside():
             carried_over(rows, distance)
 
-    def square(head, so_far):
-        value = lin[:, lanes(head)] * valid_col[...]
-        return so_far + value * value
-
-    squares = lax.fori_loop(0, heads, square, jnp.zeros((rows, TILE), jnp.float32))
+    def square(quad, so_far):
+        for head in [4 * quad + i for i in range(4)]:
+            value = lin[:, lanes(head)]
+            so_far = so_far + value * value
+        return so_far
+
+    squares = lax.fori_loop(0, heads // 4, square, jnp.zeros((rows, TILE), jnp.float32))
+    squares = squares * valid_col[...]
     square_mine[...] = lax.dot_general(
         jnp.ones((8, TILE), jnp.float32),
         squares,
@@ -421,15 +430,18 @@
     inverse = lax.rsqrt(summed * (1.0 / (features * head_size)) + norm_eps)
     enter_all[...] = jnp.broadcast_to(inverse[0:1], (TILE, rows)).T * valid_col[...]
 
-    def finish_lin(head, carry):
-        span = lanes(head)
-        opened = 0.5 + 0.5 * jnp.tanh(0.5 * gate[:, span].astype(jnp.float32))
-        lin_stage[:, span] = (lin[:, span] * enter_all[...] * gain_ref[:, span] * opened).astype(
-            jnp.bfloat16
-        )
+    def finish_lin(quad, carry):
+        made = []
+        for head in [4 * quad + i for i in range(4)]:
+            span = lanes(head)
+            opened = 0.5 + 0.5 * jnp.tanh(0.5 * gate[:, span].astype(jnp.float32))
+            value = lin[:, span] * enter_all[...] * gain_ref[:, span] * opened
+            made.append((span, value.astype(jnp.bfloat16)))
+        for span, value in made:
+            lin_stage[:, span] = value
         return carry
 
-    lax.fori_loop(0, heads, finish_lin, 0)
+    lax.fori_loop(0, heads // 4, finish_lin, 0)
     lin_store = pltpu.make_async_copy(lin_stage, lin_hbm, out_sem.at[1])
     lin_store.start()
     for distance in range(1, window + 1):

time: 43 us -> 41.4 us (0.963)
  Pallas kernels: 38.2 us -> 36.6 us
    pallas_call x1, Pallas kernels: 38.2 us -> 36.6 us  [per_device(): pl.pallas_call(functools.partial(kernel, ctx_size, head_size), out_shape=...]
where the time goes in v3:
time: 41.4 us; the launch traced here: 41.3 us
  Pallas kernels  36.6 us (88%)
  local copies, waits for them, and re-layouts  3.99 us (10%)
  between operations  0.65 us (2%)
    pallas_call x1, Pallas kernels, per_device(): pl.pallas_call(functools.partial(kernel, ctx_size, head_size), out_shape=...  36.6 us
    unnamed x4, local copies, waits for them, and re-layouts  3.99 us

profile of v3, /device:TPU:18, one launch (start us, length us, event | category | flops | bytes accessed | tf_op | source)
XLA Modules:
  0.0 41.3 jit_solution(10480684261603665694)
XLA Ops:
  0.6 36.6 %shard_map.122 = (bf16[384,2048]{1,0:T(8,128)(2,1)}, bf16[384,2048]{1,0:T(8,128)(2,1)}) custom-call(bf16[384,2048]{1,0:T(8,128)(2,1)} %lq_hbm.1, bf16[384,2048]{1,0:T(8,128)(2,1)} %lk_hbm.1, bf16[384,2048]{1,0:T(8,128)(2,1)} %lv_hbm.1, bf16[384,2048]{1,0:T(8,128)(2,1)} %gate_hbm.1, f32[16,384]{1,0:T(8,128)} %bitcast.2, f32[1,2048]{1,0:T(1,128)} %bitcast.3, ...), custom_call_target="tpu_custom_call" | custom-call | tf_op jit(solution)/shard_map/pallas_call | solution.py:514
  37.3 0.0 copy-start
  37.3 2.8 %copy.15 = bf16[384,2048]{1,0:T(8,128)(2,1)} copy(bf16[384,2048]{1,0:T(8,128)(2,1)} %get-tuple-element.4) | data formatting | bytes 3145728
  40.1 0.0 copy-done
  40.1 1.1 %copy.16 = bf16[384,2048]{1,0:T(8,128)(2,1)} copy(bf16[384,2048]{1,0:T(8,128)(2,1)S(1)} %copy-done) | data formatting | bytes 3145728
Async XLA Ops:
  37.3 2.9 %copy-start = (bf16[384,2048]{1,0:T(8,128)(2,1)S(1)}, bf16[384,2048]{1,0:T(8,128)(2,1)}, u32[]{:S(2)}) copy-start(bf16[384,2048]{1,0:T(8,128)(2,1)} %get-tuple-element.5) | copy-start | bytes 4718596

commit v4 on v3

--- a/solution.py
+++ b/solution.py
@@ -347,7 +347,7 @@
             def attend_inside():
                 attend_all(pairs_from, pairs_to, rows, distance)
 
-    attend(0, heads // 4)
+    attend(0, 3 * heads // 8)
 
     for distance in range(1, window + 1):
 
@@ -417,7 +417,7 @@
     for step in range(1, head_size):
         square_copy(step).start()
 
-    attend(heads // 4, heads // 2)
+    attend(3 * heads // 8, heads // 2)
     soft_store = pltpu.make_async_copy(soft_stage, soft_hbm, out_sem.at[0])
     soft_store.start()
 

time: 41.4 us -> 37.9 us (0.915)
  Pallas kernels: 36.6 us -> 33.1 us
    pallas_call x1, Pallas kernels: 36.6 us -> 33.1 us  [per_device(): pl.pallas_call(functools.partial(kernel, ctx_size, head_size), out_shape=...]
where the time goes in v4:
time: 37.9 us; the launch traced here: 37.7 us
  Pallas kernels  33.1 us (87%)
  local copies, waits for them, and re-layouts  3.99 us (11%)
  between operations  0.65 us (2%)
    pallas_call x1, Pallas kernels, per_device(): pl.pallas_call(functools.partial(kernel, ctx_size, head_size), out_shape=...  33.1 us
    unnamed x4, local copies, waits for them, and re-layouts  3.99 us

profile of v4, /device:TPU:18, one launch (start us, length us, event | category | flops | bytes accessed | tf_op | source)
XLA Modules:
  0.0 37.7 jit_solution(16904130271494076425)
XLA Ops:
  0.6 33.1 %shard_map.122 = (bf16[384,2048]{1,0:T(8,128)(2,1)}, bf16[384,2048]{1,0:T(8,128)(2,1)}) custom-call(bf16[384,2048]{1,0:T(8,128)(2,1)} %lq_hbm.1, bf16[384,2048]{1,0:T(8,128)(2,1)} %lk_hbm.1, bf16[384,2048]{1,0:T(8,128)(2,1)} %lv_hbm.1, bf16[384,2048]{1,0:T(8,128)(2,1)} %gate_hbm.1, f32[16,384]{1,0:T(8,128)} %bitcast.2, f32[1,2048]{1,0:T(1,128)} %bitcast.3, ...), custom_call_target="tpu_custom_call" | custom-call | tf_op jit(solution)/shard_map/pallas_call | solution.py:514
  33.7 0.0 copy-start
  33.7 2.8 %copy.15 = bf16[384,2048]{1,0:T(8,128)(2,1)} copy(bf16[384,2048]{1,0:T(8,128)(2,1)} %get-tuple-element.4) | data formatting | bytes 3145728
  36.6 0.0 copy-done
  36.6 1.1 %copy.16 = bf16[384,2048]{1,0:T(8,128)(2,1)} copy(bf16[384,2048]{1,0:T(8,128)(2,1)S(1)} %copy-done) | data formatting | bytes 3145728
Async XLA Ops:
  33.7 2.9 %copy-start = (bf16[384,2048]{1,0:T(8,128)(2,1)S(1)}, bf16[384,2048]{1,0:T(8,128)(2,1)}, u32[]{:S(2)}) copy-start(bf16[384,2048]{1,0:T(8,128)(2,1)} %get-tuple-element.5) | copy-start | bytes 4718596
